TPU v7x, 256 devices: a whole 4x4x8 slice. The times are simulated.
256 devices in a mesh: band: 64 (over x, z, y_hi), grid: 4 (over y_lo, core).
Axes of the slice: x: 4, y: 4 (y_hi: 2, y_lo: 2; y = y_hi * 2 + y_lo), z: 8, core: 2. Of those that a mesh axis runs over, the one named last changes fastest.
Arguments:
- orbitals: float32 [64, 128, 128, 128], P('band', 'grid'), may hold values from -4.6 to 4.6
Outputs:
- exchange_out: float32 [64, 128, 128, 128], P('band', 'grid')
All inputs are finite; a program needn't handle non-finite values.
Results may differ from a plain program's by a relative error of at most 0.0003.
Values sent between devices are 32-bit elements; how exact they have to be, the bound alone decides.
A program may use at most 128 MiB of HBM per device.

v0:
```python
import functools
import math

import jax
import jax.numpy as jnp
import ml_dtypes
import numpy as np
from jax import lax
from jax.experimental import pallas as pl
from jax.experimental.pallas import tpu as pltpu
from jax.sharding import PartitionSpec as P

MESH = pl.DeviceIdType.MESH
BF16 = jnp.bfloat16
F32 = jnp.float32
N = 128
Q = 32
H = 64

OH, OX, PH, PX, MH, MX, QH, QX, RH, RX = range(10)
PART = 16
CH = 2
CHUNKS = 13
ZROWS = CHUNKS * CH
EARLY = 4
(
    T_OXA, T_OXB, T_PXA, T_PXB, T_MHA, T_MHB, T_QHA, T_QHB,
    T_MXA, T_MXB, T_QXA, T_QXB, T_PHA, T_PHB, T_RXZ, T_RHZ,
) = range(16)
T_RX = 16
T_RH = T_RX + CHUNKS
T_COUNT = T_RH + CHUNKS
SETS = 3
UNROLL = 8
WIDE = 16


def split(value):
    high = value.astype(BF16)
    low = (value - high.astype(F32)).astype(BF16)
    return high, low


def mm(a, b):
    return jnp.dot(a, b, preferred_element_type=F32)


def stacked(value):
    high, low = split(value)
    return jnp.concatenate([high, low], axis=0)


def kernel(
    x_ref, wz_in, wy_in, wx_in, wxi_in, wyi_in, out_ref,
    orb, spec, send, ga, gb, back, vt, acc, wz, wy, wx, wxi, wyi,
    ssem, rsem, esem, fsem, bsem, csem, lsem,
):
    band = lax.axis_index("band")
    grid = lax.axis_index("grid")
    bands = lax.axis_size("band")
    core = grid % 2
    side = band % 2
    mate = (band, grid + 1 - 2 * core)
    near = (band, (grid + 2) % 4)
    cross = (band + 1 - 2 * side, (grid + 2) % 4)
    up = ((band + 2) % bands, grid)
    down = ((band + bands - 2) % bands, grid)
    beyond = (jnp.where(side == 0, up[0], down[0]), grid)

    fetches = [(x_ref.at[0], orb.at[OH]), (wz_in, wz), (wy_in, wy), (wx_in, wx), (wxi_in, wxi), (wyi_in, wyi)]
    fetches = [pltpu.make_async_copy(src, dst, lsem.at[i]) for i, (src, dst) in enumerate(fetches)]
    barrier = pltpu.get_barrier_semaphore()
    for other in (mate, near, cross, up, down):
        pl.semaphore_signal(barrier, inc=1, device_id=other, device_id_type=MESH)
    pl.semaphore_wait(barrier, 5)

    def remote(src, dst, send_sem, recv_sem, device):
        return pltpu.make_async_remote_copy(
            src_ref=src, dst_ref=dst, send_sem=send_sem, recv_sem=recv_sem, device_id=device, device_id_type=MESH
        )

    moves = {}

    def transfer(index, src, dst, device):
        moves[index] = remote(src, dst, ssem.at[index], rsem.at[index], device)

    def passed_on(index, src_slot, dst_slot, first, count, device):
        rows = pl.ds(first, count)
        transfer(index, orb.at[src_slot, rows], orb.at[dst_slot, rows], device)

    for index, slot, device in ((T_OXA, OX, near), (T_PXA, PX, cross), (T_MHA, MH, up), (T_QHA, QH, down)):
        for part in range(2):
            rows = pl.ds(part * PART, PART)
            transfer(index + part, x_ref.at[0, rows], orb.at[slot, rows], device)
    passed_on(T_MXA, OX, MX, 0, PART, up)
    passed_on(T_MXB, OX, MX, PART, PART, up)
    passed_on(T_QXA, OX, QX, 0, PART, down)
    passed_on(T_QXB, OX, QX, PART, PART, down)
    passed_on(T_PHA, PX, PH, 0, PART, near)
    passed_on(T_PHB, OX, PH, PART, PART, cross)
    passed_on(T_RXZ, PX, RX, ZROWS, Q - ZROWS, beyond)
    passed_on(T_RHZ, PH, RH, ZROWS, Q - ZROWS, beyond)
    far_source = jnp.where(side == 0, QH, MH)
    for k in range(CHUNKS):
        passed_on(T_RX + k, far_source, RX, k * CH, CH, cross)
        passed_on(T_RH + k, RX, RH, k * CH, CH, near)

    block = H * PART
    first_mate = jnp.where(core == 0, 6, 2) * block
    second_mate = jnp.where(core == 0, 2, 6) * block

    def swap(s, part):
        at = (first_mate if part < 2 else second_mate) + (part % 2) * block
        sem = s * 4 + part
        return remote(send.at[s, part], spec.at[s, pl.ds(at, block)], esem.at[sem], fsem.at[sem], mate)

    swaps = {(s, part): swap(s, part) for s in range(SETS) for part in range(4)}

    def give_back(turn, c):
        sem = turn * 2 + c
        return remote(back.at[turn, c], gb.at[turn, c], bsem.at[sem], csem.at[sem], mate)

    def forward(s, o_slot, j_slot, part, begin=0, end=PART // 2):
        first = (part % 2) * PART
        keep = (part % 2 + part // 2 * 4) * block

        def step(i, _):
            a = i * 2
            rho = (orb[o_slot, pl.ds(first + a, 2)] * orb[j_slot, pl.ds(first + a, 2)]).reshape(2 * N, N)
            high, low = split(rho)
            t = mm(jnp.concatenate([high, low], axis=1), wz[...])
            t = t[:, :N] + t[:, N:]
            u = mm(wy[core], stacked(jnp.concatenate([t[:N], t[N:]], axis=1)))
            u = u[:N] + u[N:]
            for b in range(2):
                plane = u[:, b * N : b * N + N]
                spec[s, pl.ds(keep + a + b, H, stride=PART), :] = plane[:H]
                send[s, part, pl.ds(a + b, H, stride=PART), :] = plane[H:]
            return 0

        lax.fori_loop(begin, end, step, 0, unroll=end - begin)
        if end == PART // 2:
            swaps[s, part].start()

    def row_of(s, k):
        return jnp.concatenate(
            [spec[s, pl.ds(pl.multiple_of(p * block + k * PART, PART), PART), :] for p in range(8)], axis=0
        )

    def along_x(s, turn):
        column = row_of(s, 0)
        column = column - jnp.where(zero_mode, jnp.mean(column, axis=0, keepdims=True), 0.0)
        for p in range(8):
            spec[s, pl.ds(p * block, PART), :] = column[p * PART : p * PART + PART]

        def half(c, _):
            def step(i, _):
                k = c * (H // 2) + i * WIDE
                m = jnp.concatenate([row_of(s, k + b) for b in range(WIDE)], axis=1)
                f = mm(wx[...], stacked(m))
                v = jnp.concatenate([vt[pl.ds(pl.multiple_of((k + b) * N, N), N), :] for b in range(WIDE)], axis=1)
                f = (f[:N] + f[N:]) * v
                r = mm(wxi[core], stacked(f))
                r = r[:H] + r[H:]
                for b in range(WIDE):
                    plane = r[:, b * N : b * N + N]
                    ga[turn, c, pl.ds(i * WIDE + b, Q, stride=H // 2), :] = plane[:Q]
                    back[turn, c, pl.ds(i * WIDE + b, Q, stride=H // 2), :] = plane[Q:]
                return 0

            lax.fori_loop(0, H // 2 // WIDE, step, 0, unroll=2)
            give_back(turn, c).start()
            return 0

        lax.fori_loop(0, 2, half, 0)

    def inverse(j_slot, turn, first=False, last=False):
        give_back(turn, 0).wait()
        give_back(turn, 1).wait()

        def step(i, _):
            a = i * 2
            planes = []
            for b in range(2):
                rows = pl.ds(pl.multiple_of((a + b) * (H // 2), H // 2), H // 2)
                planes.append(
                    jnp.concatenate([ga[turn, 0, rows, :], ga[turn, 1, rows, :], gb[turn, 0, rows, :], gb[turn, 1, rows, :]], axis=0)
                )
            t = mm(wyi[core], stacked(jnp.concatenate(planes, axis=1)))
            t = t[:N] + t[N:]
            high, low = split(jnp.concatenate([t[:, :N], t[:, N:]], axis=0))
            w = mm(jnp.concatenate([high, low], axis=1), wz[...])
            w = (w[:, :N] + w[:, N:]).reshape(2, N, N) * orb[j_slot, pl.ds(a, 2)]
            if first:
                acc[pl.ds(a, 2)] = w
            else:
                acc[pl.ds(a, 2)] += w
            return 0

        if not last:
            lax.fori_loop(0, Q // 2, step, 0, unroll=UNROLL)
            return
        stores = []
        for part in range(2):
            lax.fori_loop(part * PART // 2, (part + 1) * PART // 2, step, 0, unroll=PART // 2)
            rows = pl.ds(part * PART, PART)
            stores.append(pltpu.make_async_copy(acc.at[rows], out_ref.at[0, rows], lsem.at[part]))
            stores[part].start()
        for store in stores:
            store.wait()

    def spectrum(s, turn):
        for part in (2, 3, 0, 1):
            swaps[s, part].wait()
        along_x(s, turn)

    def arrived(*indices):
        for t in indices:
            moves[t].wait_recv()

    def start(*indices):
        for t in indices:
            moves[t].start()

    def pass_on(*chunks):
        for k in chunks:
            arrived(T_RX + k)
            start(T_RH + k)

    start(T_OXA, T_PXA, T_MHA, T_QHA, T_OXB, T_PXB, T_MHB, T_QHB)
    for fetch in fetches:
        fetch.start()

    strength = N * math.sqrt(N) / 16.0 / float(N**3)
    row = lax.broadcasted_iota(jnp.int32, (N, N), 0)
    column = lax.broadcasted_iota(jnp.int32, (N, N), 1)
    row = jnp.minimum(row, N - row)
    column = jnp.minimum(column, N - column)
    plane = row * row + column * column
    zero_mode = jnp.logical_and(lax.broadcasted_iota(jnp.int32, (1, N), 1) == 0, core == 0)

    def table(i, _):
        ky = core * H + i
        ky = jnp.minimum(ky, N - ky)
        d = (plane + ky * ky).astype(F32)
        vt[pl.ds(pl.multiple_of(i * N, N), N), :] = jnp.where(d > 0, strength / jnp.maximum(d, 1.0), 0.0)
        return 0

    lax.fori_loop(0, H, table, 0)
    for fetch in fetches:
        fetch.wait()
    forward(0, OH, OH, 0)
    forward(0, OH, OH, 1)

    arrived(T_OXA)
    start(T_MXA, T_QXA)
    arrived(T_PXA)
    start(T_PHA)
    arrived(T_MHA, T_QHA)
    start(*range(T_RX, T_RX + EARLY))
    forward(0, OX, OX, 2)
    forward(1, OH, MH, 0)
    forward(2, OH, QH, 0)
    arrived(T_OXB)
    start(T_MXB, T_QXB, T_PHB)
    arrived(T_PXB)
    start(T_RXZ)
    arrived(T_MHB, T_QHB)
    start(*range(T_RX + EARLY, T_RX + CHUNKS))
    forward(0, OX, OX, 3)
    forward(1, OH, MH, 1)
    forward(2, OH, QH, 1)
    spectrum(0, 0)
    pass_on(0, 1)
    inverse(OH, 0, first=True)
    pass_on(2, 3)
    forward(0, OX, PX, 2)
    forward(0, OX, PX, 3)
    arrived(T_PHA)
    forward(0, OH, PH, 0)
    arrived(T_MXA)
    forward(1, OX, MX, 2)
    arrived(T_QXA)
    forward(2, OX, QX, 2)
    arrived(T_PHB)
    start(T_RHZ)
    forward(0, OH, PH, 1)
    pass_on(4)
    spectrum(0, 1)
    pass_on(5)
    inverse(PH, 1)
    pass_on(6, 7)
    forward(0, OX, RX, 2)
    arrived(T_MXB)
    forward(1, OX, MX, 3)
    arrived(T_QXB)
    forward(2, OX, QX, 3)
    spectrum(1, 0)
    pass_on(8)
    spectrum(2, 1)
    pass_on(9)
    inverse(MH, 0)
    pass_on(10)
    inverse(QH, 1)
    pass_on(11)
    arrived(*range(T_RH, T_RH + 8))
    forward(0, OH, RH, 0)
    pass_on(12)
    over_z = (ZROWS - PART) // 2
    forward(0, OX, RX, 3, end=over_z)
    arrived(T_RXZ)
    forward(0, OX, RX, 3, begin=over_z)
    arrived(*range(T_RH + 8, T_RH + CHUNKS))
    forward(0, OH, RH, 1, end=over_z)
    arrived(T_RHZ)
    forward(0, OH, RH, 1, begin=over_z)
    spectrum(0, 0)
    inverse(RH, 0, last=True)
    for t in range(T_COUNT):
        moves[t].wait_send()


def halves(matrix):
    high = matrix.astype(ml_dtypes.bfloat16)
    low = (matrix - high.astype(np.float64)).astype(ml_dtypes.bfloat16)
    return high, low


def left_weight(matrix):
    high, low = halves(matrix)
    return np.concatenate(
        [np.concatenate([high, high], axis=1), np.concatenate([low, np.zeros_like(low)], axis=1)], axis=0
    )


def tables():
    index = np.arange(N)
    angle = 2.0 * np.pi / N * (index[:, None] * index[None, :] % N)
    cas = np.cos(angle) + np.sin(angle)
    high, low = halves(cas)
    wz = np.concatenate(
        [np.concatenate([high, low], axis=1), np.concatenate([high, np.zeros_like(low)], axis=1)], axis=0
    )
    order = [np.concatenate([index[c * H : c * H + H], index[H - c * H : N - c * H]]) for c in (0, 1)]
    wy = np.stack([left_weight(cas[order[c]]) for c in (0, 1)])
    wyi = np.stack([left_weight(cas[:, order[c]]) for c in (0, 1)])
    wx = left_weight(cas)
    kept = [np.concatenate([index[:Q], index[Q : 2 * Q]]), np.concatenate([index[:Q], index[3 * Q :]])]
    wxi = np.stack([left_weight(cas[kept[c]]) for c in (0, 1)])
    return wz, wy, wx, wxi, wyi


def on_device(orbitals):
    weights = [jnp.asarray(w) for w in tables()]
    total = pl.pallas_call(
        kernel,
        out_shape=jax.ShapeDtypeStruct(orbitals.shape, F32),
        in_specs=[pl.BlockSpec(memory_space=pl.ANY)] * 6,
        out_specs=pl.BlockSpec(memory_space=pl.ANY),
        scratch_shapes=[
            pltpu.VMEM((10, Q, N, N), F32),
            pltpu.VMEM((SETS, N * H, N), F32),
            pltpu.VMEM((SETS, 4, H * PART, N), F32),
            pltpu.VMEM((2, 2, Q * H // 2, N), F32),
            pltpu.VMEM((2, 2, Q * H // 2, N), F32),
            pltpu.VMEM((2, 2, Q * H // 2, N), F32),
            pltpu.VMEM((H * N, N), F32),
            pltpu.VMEM((Q, N, N), F32),
        ]
        + [pltpu.VMEM(w.shape, BF16) for w in weights]
        + [pltpu.SemaphoreType.DMA((n,)) for n in (T_COUNT, T_COUNT, SETS * 4, SETS * 4, 4, 4, 6)],
        compiler_params=pltpu.CompilerParams(
            collective_id=0, has_side_effects=True, vmem_limit_bytes=60 * 1024 * 1024
        ),
    )(orbitals, *weights)
    return -total


def solution(mesh):
    spec = P("band", "grid", None, None)
    return jax.shard_map(on_device, mesh=mesh, in_specs=(spec,), out_specs=spec, check_vma=False)
```

profile of v0, /device:TPU:1, one launch (start us, length us, event | category | flops | bytes accessed | tf_op | source)
XLA Modules:
  0.0 140.8 jit_solution(863104537365806419)
XLA Ops:
  0.0 137.6 %shard_map.64 = f32[1,32,128,128]{3,2,1,0:T(8,128)} custom-call(f32[1,32,128,128]{3,2,1,0:T(8,128)} %x_ref.1, bf16[256,256]{1,0:T(8,128)(2,1)} %constant.10.clone.wz_in, bf16[2,256,256]{2,1,0:T(8,128)(2,1)} %constant.11.clone.wy_in, bf16[256,256]{1,0:T(8,128)(2,1)} %constant.12.clone.wx_in, bf16[2,128,256]{2,1,0:T(8,128)(2,1)} %constant.13.clone.wxi_in, ...), custom_call_target="tpu_custom_call" | custom-call | tf_op jit(solution)/shard_map/pallas_call | solution.py:355
  137.6 3.1 %neg.3 = f32[1,32,128,128]{3,2,1,0:T(8,128)} negate(f32[1,32,128,128]{3,2,1,0:T(8,128)} %shard_map.64) | non-fusion elementwise | flops 524288 | bytes 4194304 | tf_op jit(solution)/shard_map/neg | solution.py:376
where the time goes:
time: 141 us
  Pallas kernels  138 us (98%)
  other arithmetic  3.14 us (2%)
    pallas_call x1, Pallas kernels, on_device(): pl.pallas_call(kernel, out_shape=jax.ShapeDtypeStruct(orbitals.shape, F32...  138 us
    neg x1, other arithmetic, on_device(): return -total  3.14 us

commit v1 on v0

--- a/solution.py
+++ b/solution.py
@@ -25,11 +25,12 @@
 EARLY = 4
 (
     T_OXA, T_OXB, T_PXA, T_PXB, T_MHA, T_MHB, T_QHA, T_QHB,
-    T_MXA, T_MXB, T_QXA, T_QXB, T_PHA, T_PHB, T_RXZ, T_RHZ,
-) = range(16)
-T_RX = 16
+    T_MXA, T_MXB, T_QXA, T_QXB, T_PHA, T_PHB, T_PHC, T_RXZ, T_RHZ,
+) = range(17)
+T_RX = 17
 T_RH = T_RX + CHUNKS
 T_COUNT = T_RH + CHUNKS
+NEAR_ROWS = 18
 SETS = 3
 UNROLL = 8
 WIDE = 16
@@ -97,7 +98,8 @@
     passed_on(T_QXA, OX, QX, 0, PART, down)
     passed_on(T_QXB, OX, QX, PART, PART, down)
     passed_on(T_PHA, PX, PH, 0, PART, near)
-    passed_on(T_PHB, OX, PH, PART, PART, cross)
+    passed_on(T_PHC, PX, PH, PART, NEAR_ROWS - PART, near)
+    passed_on(T_PHB, OX, PH, NEAR_ROWS, Q - NEAR_ROWS, cross)
     passed_on(T_RXZ, PX, RX, ZROWS, Q - ZROWS, beyond)
     passed_on(T_RHZ, PH, RH, ZROWS, Q - ZROWS, beyond)
     far_source = jnp.where(side == 0, QH, MH)
@@ -261,12 +263,13 @@
     forward(0, OX, OX, 2)
     forward(1, OH, MH, 0)
     forward(2, OH, QH, 0)
+    arrived(T_PXB)
+    start(T_PHC)
     arrived(T_OXB)
     start(T_MXB, T_QXB, T_PHB)
-    arrived(T_PXB)
-    start(T_RXZ)
     arrived(T_MHB, T_QHB)
     start(*range(T_RX + EARLY, T_RX + CHUNKS))
+    start(T_RXZ)
     forward(0, OX, OX, 3)
     forward(1, OH, MH, 1)
     forward(2, OH, QH, 1)
@@ -276,36 +279,35 @@
     pass_on(2, 3)
     forward(0, OX, PX, 2)
     forward(0, OX, PX, 3)
-    arrived(T_PHA)
-    forward(0, OH, PH, 0)
     arrived(T_MXA)
     forward(1, OX, MX, 2)
     arrived(T_QXA)
     forward(2, OX, QX, 2)
-    arrived(T_PHB)
+    arrived(T_PHA)
+    forward(0, OH, PH, 0)
+    arrived(T_PHC, T_PHB)
     start(T_RHZ)
     forward(0, OH, PH, 1)
+    spectrum(0, 1)
     pass_on(4)
-    spectrum(0, 1)
-    pass_on(5)
     inverse(PH, 1)
-    pass_on(6, 7)
+    pass_on(5, 6, 7)
     forward(0, OX, RX, 2)
     arrived(T_MXB)
     forward(1, OX, MX, 3)
+    pass_on(8)
     arrived(T_QXB)
     forward(2, OX, QX, 3)
     spectrum(1, 0)
-    pass_on(8)
+    pass_on(9)
     spectrum(2, 1)
-    pass_on(9)
+    pass_on(10)
     inverse(MH, 0)
-    pass_on(10)
+    pass_on(11)
     inverse(QH, 1)
-    pass_on(11)
+    pass_on(12)
     arrived(*range(T_RH, T_RH + 8))
     forward(0, OH, RH, 0)
-    pass_on(12)
     over_z = (ZROWS - PART) // 2
     forward(0, OX, RX, 3, end=over_z)
     arrived(T_RXZ)
@@ -354,7 +356,7 @@
     weights = [jnp.asarray(w) for w in tables()]
     total = pl.pallas_call(
         kernel,
-        out_shape=jax.ShapeDtypeStruct(orbitals.shape, F32),
+        out_shape=pltpu.VMEM(orbitals.shape, F32),
         in_specs=[pl.BlockSpec(memory_space=pl.ANY)] * 6,
         out_specs=pl.BlockSpec(memory_space=pl.ANY),
         scratch_shapes=[

time: 141 us -> 135 us (0.957)
  Pallas kernels: 138 us -> 133 us
  other arithmetic: 3.14 us -> 1.55 us
    pallas_call x1, Pallas kernels: 138 us -> 133 us  [on_device(): pl.pallas_call(kernel, out_shape=pltpu.VMEM(orbitals.shape, F32), in_spec...]
    neg x1, other arithmetic: 3.14 us -> 1.55 us  [on_device(): return -total]
where the time goes in v1:
time: 135 us
  Pallas kernels  133 us (99%)
  other arithmetic  1.55 us (1%)
    pallas_call x1, Pallas kernels, on_device(): pl.pallas_call(kernel, out_shape=pltpu.VMEM(orbitals.shape, F32), in_spec...  133 us

profile of v1, /device:TPU:1, one launch (start us, length us, event | category | flops | bytes accessed | tf_op | source)
XLA Modules:
  0.0 134.9 jit_solution(5143386359223296415)
XLA Ops:
  0.0 133.3 %shard_map.64 = f32[1,32,128,128]{3,2,1,0:T(8,128)S(1)} custom-call(f32[1,32,128,128]{3,2,1,0:T(8,128)} %x_ref.1, bf16[256,256]{1,0:T(8,128)(2,1)} %constant.10.clone.wz_in, bf16[2,256,256]{2,1,0:T(8,128)(2,1)} %constant.11.clone.wy_in, bf16[256,256]{1,0:T(8,128)(2,1)} %constant.12.clone.wx_in, bf16[2,128,256]{2,1,0:T(8,128)(2,1)} %constant.13.clone.wxi_in, ...), custom_call_target="tpu_custom_call" | custom-call | tf_op jit(solution)/shard_map/pallas_call | solution.py:357
  133.3 1.6 %neg.3 = f32[1,32,128,128]{3,2,1,0:T(8,128)} negate(f32[1,32,128,128]{3,2,1,0:T(8,128)S(1)} %shard_map.64) | non-fusion elementwise | flops 524288 | bytes 4194304 | tf_op jit(solution)/shard_map/neg | solution.py:378

commit v2 on v1

--- a/solution.py
+++ b/solution.py
@@ -176,9 +176,10 @@
 
         lax.fori_loop(0, 2, half, 0)
 
-    def inverse(j_slot, turn, first=False, last=False):
-        give_back(turn, 0).wait()
-        give_back(turn, 1).wait()
+    def inverse(j_slot, turn, first=False, last=False, parts=(0, 1)):
+        if 0 in parts:
+            give_back(turn, 0).wait()
+            give_back(turn, 1).wait()
 
         def step(i, _):
             a = i * 2
@@ -199,15 +200,13 @@
                 acc[pl.ds(a, 2)] += w
             return 0
 
-        if not last:
-            lax.fori_loop(0, Q // 2, step, 0, unroll=UNROLL)
-            return
         stores = []
-        for part in range(2):
-            lax.fori_loop(part * PART // 2, (part + 1) * PART // 2, step, 0, unroll=PART // 2)
-            rows = pl.ds(part * PART, PART)
-            stores.append(pltpu.make_async_copy(acc.at[rows], out_ref.at[0, rows], lsem.at[part]))
-            stores[part].start()
+        for part in parts:
+            lax.fori_loop(part * PART // 2, (part + 1) * PART // 2, step, 0, unroll=UNROLL)
+            if last:
+                rows = pl.ds(part * PART, PART)
+                stores.append(pltpu.make_async_copy(acc.at[rows], out_ref.at[0, rows], lsem.at[part]))
+                stores[part].start()
         for store in stores:
             store.wait()
 
@@ -304,10 +303,9 @@
     pass_on(10)
     inverse(MH, 0)
     pass_on(11)
-    inverse(QH, 1)
-    pass_on(12)
     arrived(*range(T_RH, T_RH + 8))
     forward(0, OH, RH, 0)
+    pass_on(12)
     over_z = (ZROWS - PART) // 2
     forward(0, OX, RX, 3, end=over_z)
     arrived(T_RXZ)
@@ -316,7 +314,9 @@
     forward(0, OH, RH, 1, end=over_z)
     arrived(T_RHZ)
     forward(0, OH, RH, 1, begin=over_z)
+    inverse(QH, 1, parts=(0,))
     spectrum(0, 0)
+    inverse(QH, 1, parts=(1,))
     inverse(RH, 0, last=True)
     for t in range(T_COUNT):
         moves[t].wait_send()

time: 135 us -> 135 us (level)
  no operation moved by 1% of the time
where the time goes in v2:
time: 135 us
  Pallas kernels  133 us (99%)
  other arithmetic  1.55 us (1%)
    pallas_call x1, Pallas kernels, on_device(): pl.pallas_call(kernel, out_shape=pltpu.VMEM(orbitals.shape, F32), in_spec...  133 us

profile of v2, /device:TPU:1, one launch (start us, length us, event | category | flops | bytes accessed | tf_op | source)
XLA Modules:
  0.0 134.9 jit_solution(18353581342385021497)
XLA Ops:
  0.0 133.4 %shard_map.64 = f32[1,32,128,128]{3,2,1,0:T(8,128)S(1)} custom-call(f32[1,32,128,128]{3,2,1,0:T(8,128)} %x_ref.1, bf16[256,256]{1,0:T(8,128)(2,1)} %constant.10.clone.wz_in, bf16[2,256,256]{2,1,0:T(8,128)(2,1)} %constant.11.clone.wy_in, bf16[256,256]{1,0:T(8,128)(2,1)} %constant.12.clone.wx_in, bf16[2,128,256]{2,1,0:T(8,128)(2,1)} %constant.13.clone.wxi_in, ...), custom_call_target="tpu_custom_call" | custom-call | tf_op jit(solution)/shard_map/pallas_call | solution.py:357
  133.4 1.6 %neg.3 = f32[1,32,128,128]{3,2,1,0:T(8,128)} negate(f32[1,32,128,128]{3,2,1,0:T(8,128)S(1)} %shard_map.64) | non-fusion elementwise | flops 524288 | bytes 4194304 | tf_op jit(solution)/shard_map/neg | solution.py:378

commit v3 on v2

--- a/solution.py
+++ b/solution.py
@@ -149,7 +149,7 @@
             [spec[s, pl.ds(pl.multiple_of(p * block + k * PART, PART), PART), :] for p in range(8)], axis=0
         )
 
-    def along_x(s, turn):
+    def along_x(s, turn, chunk):
         column = row_of(s, 0)
         column = column - jnp.where(zero_mode, jnp.mean(column, axis=0, keepdims=True), 0.0)
         for p in range(8):
@@ -172,6 +172,12 @@
 
             lax.fori_loop(0, H // 2 // WIDE, step, 0, unroll=2)
             give_back(turn, c).start()
+            if chunk is not None:
+
+                @pl.when(c == 0)
+                def _():
+                    pass_on(chunk)
+
             return 0
 
         lax.fori_loop(0, 2, half, 0)
@@ -210,10 +216,10 @@
         for store in stores:
             store.wait()
 
-    def spectrum(s, turn):
+    def spectrum(s, turn, chunk=None):
         for part in (2, 3, 0, 1):
             swaps[s, part].wait()
-        along_x(s, turn)
+        along_x(s, turn, chunk)
 
     def arrived(*indices):
         for t in indices:
@@ -287,22 +293,22 @@
     arrived(T_PHC, T_PHB)
     start(T_RHZ)
     forward(0, OH, PH, 1)
-    spectrum(0, 1)
-    pass_on(4)
-    inverse(PH, 1)
-    pass_on(5, 6, 7)
+    spectrum(0, 1, chunk=4)
+    inverse(PH, 1, parts=(0,))
+    pass_on(5)
+    inverse(PH, 1, parts=(1,))
+    pass_on(6, 7)
     forward(0, OX, RX, 2)
     arrived(T_MXB)
     forward(1, OX, MX, 3)
     pass_on(8)
     arrived(T_QXB)
     forward(2, OX, QX, 3)
-    spectrum(1, 0)
-    pass_on(9)
-    spectrum(2, 1)
-    pass_on(10)
-    inverse(MH, 0)
+    spectrum(1, 0, chunk=9)
+    spectrum(2, 1, chunk=10)
+    inverse(MH, 0, parts=(0,))
     pass_on(11)
+    inverse(MH, 0, parts=(1,))
     arrived(*range(T_RH, T_RH + 8))
     forward(0, OH, RH, 0)
     pass_on(12)

time: 135 us -> 134 us (level)
  no operation moved by 1% of the time
where the time goes in v3:
time: 134 us
  Pallas kernels  132 us (99%)
  other arithmetic  1.55 us (1%)
    pallas_call x1, Pallas kernels, on_device(): pl.pallas_call(kernel, out_shape=pltpu.VMEM(orbitals.shape, F32), in_spec...  132 us

profile of v3, /device:TPU:1, one launch (start us, length us, event | category | flops | bytes accessed | tf_op | source)
XLA Modules:
  0.0 134.0 jit_solution(4207969270629151471)
XLA Ops:
  0.0 132.4 %shard_map.64 = f32[1,32,128,128]{3,2,1,0:T(8,128)S(1)} custom-call(f32[1,32,128,128]{3,2,1,0:T(8,128)} %x_ref.1, bf16[256,256]{1,0:T(8,128)(2,1)} %constant.10.clone.wz_in, bf16[2,256,256]{2,1,0:T(8,128)(2,1)} %constant.11.clone.wy_in, bf16[256,256]{1,0:T(8,128)(2,1)} %constant.12.clone.wx_in, bf16[2,128,256]{2,1,0:T(8,128)(2,1)} %constant.13.clone.wxi_in, ...), custom_call_target="tpu_custom_call" | custom-call | tf_op jit(solution)/shard_map/pallas_call | solution.py:363
  132.4 1.6 %neg.3 = f32[1,32,128,128]{3,2,1,0:T(8,128)} negate(f32[1,32,128,128]{3,2,1,0:T(8,128)S(1)} %shard_map.64) | non-fusion elementwise | flops 524288 | bytes 4194304 | tf_op jit(solution)/shard_map/neg | solution.py:384

commit v4 on v3

--- a/solution.py
+++ b/solution.py
@@ -30,7 +30,7 @@
 T_RX = 17
 T_RH = T_RX + CHUNKS
 T_COUNT = T_RH + CHUNKS
-NEAR_ROWS = 18
+NEAR_ROWS = 17
 SETS = 3
 UNROLL = 8
 WIDE = 16

time: 134 us -> 135 us (level)
  Pallas kernels: 132 us -> 134 us
    pallas_call x1, Pallas kernels: 132 us -> 134 us  [on_device(): pl.pallas_call(kernel, out_shape=pltpu.VMEM(orbitals.shape, F32), in_spec...]
where the time goes in v4:
time: 135 us
  Pallas kernels  134 us (99%)
  other arithmetic  1.55 us (1%)
    pallas_call x1, Pallas kernels, on_device(): pl.pallas_call(kernel, out_shape=pltpu.VMEM(orbitals.shape, F32), in_spec...  134 us

profile of v4, /device:TPU:1, one launch (start us, length us, event | category | flops | bytes accessed | tf_op | source)
XLA Modules:
  0.0 135.4 jit_solution(682625275564794904)
XLA Ops:
  0.0 133.8 %shard_map.64 = f32[1,32,128,128]{3,2,1,0:T(8,128)S(1)} custom-call(f32[1,32,128,128]{3,2,1,0:T(8,128)} %x_ref.1, bf16[256,256]{1,0:T(8,128)(2,1)} %constant.10.clone.wz_in, bf16[2,256,256]{2,1,0:T(8,128)(2,1)} %constant.11.clone.wy_in, bf16[256,256]{1,0:T(8,128)(2,1)} %constant.12.clone.wx_in, bf16[2,128,256]{2,1,0:T(8,128)(2,1)} %constant.13.clone.wxi_in, ...), custom_call_target="tpu_custom_call" | custom-call | tf_op jit(solution)/shard_map/pallas_call | solution.py:363
  133.8 1.6 %neg.3 = f32[1,32,128,128]{3,2,1,0:T(8,128)} negate(f32[1,32,128,128]{3,2,1,0:T(8,128)S(1)} %shard_map.64) | non-fusion elementwise | flops 524288 | bytes 4194304 | tf_op jit(solution)/shard_map/neg | solution.py:384
